TPU v7x, 256 devices: a whole 4x4x8 slice. The times are simulated.
256 devices in a mesh: lsec: 16 (over x, z_lo), rsec: 16 (over z_hi, y, core).
Axes of the slice: x: 4, y: 4, z: 8 (z_hi: 2, z_lo: 4; z = z_hi * 4 + z_lo), core: 2. Of those that a mesh axis runs over, the one named last changes fastest.
Arguments:
- states: float32 [2, 10240, 10240], P(None, 'lsec', 'rsec'), may hold values from -6 to 6
- left_env: float32 [16, 640, 640], P('lsec', 'rsec'), may hold values from -0.25 to 0.25
- right_env: float32 [16, 640, 640], P('rsec', 'lsec'), may hold values from -0.25 to 0.25
- left_op: float32 [16, 640, 640], P('lsec', 'rsec'), may hold values from -0.25 to 0.25
- right_op: float32 [16, 640, 640], P('rsec', 'lsec'), may hold values from -0.25 to 0.25
- sizes_left: int32 [16], P('lsec'), may hold values from 320 to 640
- sizes_right: int32 [16], P('rsec'), may hold values from 320 to 640
Outputs:
- applied: float32 [2, 10240, 10240], P(None, 'lsec', 'rsec')
All inputs are finite; a program needn't handle non-finite values.
Results may differ from a plain program's by a relative error of at most 0.000059.
Values sent between devices are 32-bit elements; how exact they have to be, the bound alone decides.
A program may use at most 128 MiB of HBM per device.

v0:
```python
import jax
import jax.numpy as jnp
from jax import lax
from jax.sharding import PartitionSpec as P

HI = lax.Precision.HIGH


def shifted(value, step):
    n, m = (lax.axis_size("lsec"), lax.axis_size("rsec"))
    pairs = [
        (i * m + j, (i + step) * m + j - step)
        for i in range(n)
        for j in range(m)
        if 0 <= i + step < n and 0 <= j - step < m
    ]
    return lax.ppermute(value, ("lsec", "rsec"), pairs)


def on_device(states, left_env, right_env, left_op, right_op, sizes_left, sizes_right):
    width = states.shape[1]
    rows = jnp.arange(width, dtype=jnp.int32)
    mask = (rows[:, None] < sizes_left[0]).astype(jnp.float32) * (
        rows[None, :] < sizes_right[0]
    ).astype(jnp.float32)
    masked = states * mask[None]
    moved = shifted(masked, 1)
    left = lax.all_gather(jnp.concatenate([left_env, left_op]), "rsec", axis=1, tiled=True)
    right = lax.all_gather(jnp.concatenate([right_env, right_op]), "lsec", axis=1, tiled=True)
    env_l, oper_l, env_r, oper_r = (left[0], left[1], right[0], right[1])
    right_part = jnp.einsum("rbc,cd->rbd", masked, oper_r, precision=HI)
    source = jnp.einsum("ba,rbd->rad", oper_l, right_part, precision=HI)
    back = shifted(source, -1)
    local = jnp.einsum("ab,rbc->rac", env_l, masked, precision=HI)
    local = local + jnp.einsum("rbc,dc->rbd", masked, env_r, precision=HI)
    inner = jnp.einsum("rbc,dc->rbd", moved, oper_r, precision=HI)
    hop = jnp.einsum("ab,rbd->rad", oper_l, inner, precision=HI)
    return (local + hop + back) * mask[None]


def solution(mesh):
    in_specs = (
        P(None, "lsec", "rsec"),
        P("lsec", "rsec", None),
        P("rsec", "lsec", None),
        P("lsec", "rsec", None),
        P("rsec", "lsec", None),
        P("lsec"),
        P("rsec"),
    )
    out_specs = P(None, "lsec", "rsec")
    return jax.shard_map(
        on_device, mesh=mesh, in_specs=in_specs, out_specs=out_specs, check_vma=False
    )
```

profile of v0, /device:TPU:198, one launch (start us, length us, event | category | flops | bytes accessed | tf_op | source)
XLA Modules:
  0.0 410.6 jit_solution(3178163259722050696)
XLA Ops:
  6.5 0.0 all-gather.5.cloned.1.call-start
  6.5 1.6 pad_maximum_fusion.1
  8.2 0.0 all-gather.5.cloned.1.call-update
  8.2 0.0 all-gather.3.cloned.1.call-start
  8.2 1.7 pad_maximum_fusion
  9.9 0.0 all-gather.3.cloned.1.call-update
  11.2 4.6 %copy.8 = f32[2,640,640]{1,2,0:T(8,128)} copy(f32[2,640,640]{2,1,0:T(8,128)} %param.7) | data formatting | bytes 6553600 | tf_op args[0]
  15.8 0.2 broadcast_multiply_fusion.1
  16.0 0.0 copy-start
  16.0 2.8 broadcast_multiply_fusion
  18.8 0.0 copy-done
  18.8 4.8 %collective-permute-start = (f32[2,640,640]{1,2,0:T(8,128)S(1)}, f32[2,640,640]{1,2,0:T(8,128)}, u32[]{:S(2)}, u32[]{:S(2)}) collective-permute-start(f32[2,640,640]{1,2,0:T(8,128)S(1)} %broadcast_multiply_fusion), channel_id=1, source_target_pairs={{1,16},{2,17},{3,18},{4,19},{5,20},{6,21},{7,22},{8,23},{9,24},{10... | collective-permute-start | bytes 9830408 | tf_op jit(solution)/shard_map/ppermute | solution.py:17
  23.6 150.1 %all-gather.5.cloned.1.call-done = f32[2,640,640]{2,1,0:T(8,128)} async-done(((f32[2,40,640]{2,1,0:T(8,128)}), f32[2,640,640]{2,1,0:T(8,128)}) %all-gather.5.cloned.1.call-update) | async-done | bytes 3276816 | tf_op jit(solution)/shard_map/all_gather | solution.py:29
  173.7 7.4 %fusion.4 = f32[2,640,640]{1,2,0:T(8,128)} fusion(f32[2,640,640]{1,2,0:T(8,128)S(1)} %broadcast_multiply_fusion, f32[2,640,640]{2,1,0:T(8,128)} %all-gather.5.cloned.1.call-done), kind=kOutput, calls=%fused_computation.12 | convolution fusion | flops 3145728000 | bytes 8192000 | tf_op jit(solution)/shard_map/rbc,cd->rbd/dot_general | solution.py:31
  181.1 83.2 %all-gather.3.cloned.1.call-done = f32[2,640,640]{2,1,0:T(8,128)} async-done(((f32[2,40,640]{2,1,0:T(8,128)}), f32[2,640,640]{2,1,0:T(8,128)}) %all-gather.3.cloned.1.call-update) | async-done | bytes 3276816 | tf_op jit(solution)/shard_map/all_gather | solution.py:28
  264.3 0.0 copy-start.3
  264.3 7.3 %convolution_bitcast_fusion = f32[2,640,640]{1,2,0:T(8,128)S(1)} fusion(f32[2,640,640]{1,2,0:T(8,128)} %fusion.4, f32[2,640,640]{2,1,0:T(8,128)} %all-gather.3.cloned.1.call-done), kind=kOutput, calls=%fused_computation.4 | convolution fusion | flops 3145728000 | bytes 8192000 | tf_op jit(solution)/shard_map/ba,rbd->rad/dot_general | solution.py:32
  271.6 0.0 copy-start.2
  271.6 2.4 collective-permute-start.1
  274.0 0.0 copy-done.3
  274.0 4.5 %fusion.2 = f32[2,640,640]{1,2,0:T(8,128)S(1)} fusion(f32[2,640,640]{1,2,0:T(8,128)S(1)} %broadcast_multiply_fusion, f32[2,640,640]{2,1,0:T(8,128)S(1)} %copy-done.3), kind=kOutput, calls=%fused_computation.8 | convolution fusion | flops 3145728000 | bytes 8192000 | tf_op jit(solution)/shard_map/rbc,dc->rbd/dot_general | solution.py:35
  278.5 0.0 copy-done.2
  278.5 4.8 %fusion.3 = f32[2,640,640]{2,1,0:T(8,128)S(1)} fusion(f32[2,640,640]{1,2,0:T(8,128)S(1)} %broadcast_multiply_fusion, f32[2,640,640]{2,1,0:T(8,128)S(1)} %copy-done.2), kind=kOutput, calls=%fused_computation.10 | convolution fusion | flops 3145728000 | bytes 8192000 | tf_op jit(solution)/shard_map/ab,rbc->rac/dot_general | solution.py:34
  283.3 0.0 copy-start.1
  283.3 0.0 collective-permute-done
  283.3 6.8 %fusion.5 = f32[2,640,640]{1,2,0:T(8,128)S(1)} fusion(f32[2,640,640]{1,2,0:T(8,128)} %collective-permute-done, f32[2,640,640]{2,1,0:T(8,128)S(1)} %copy-done.3), kind=kOutput, calls=%fused_computation.13 | convolution fusion | flops 3145728000 | bytes 8192000 | tf_op jit(solution)/shard_map/rbc,dc->rbd/dot_general | solution.py:36
  290.1 105.5 %collective-permute-done.1 = f32[2,640,640]{1,2,0:T(8,128)S(1)} collective-permute-done((f32[2,640,640]{1,2,0:T(8,128)S(1)}, f32[2,640,640]{1,2,0:T(8,128)S(1)}, u32[]{:S(2)}, u32[]{:S(2)}) %collective-permute-start.1) | collective-permute-done | bytes 3276832 | tf_op jit(solution)/shard_map/ppermute | solution.py:17
  395.6 0.0 copy-done.1
  395.6 5.2 %fusion.1 = f32[2,640,640]{1,2,0:T(8,128)S(1)} fusion(f32[2,640,640]{1,2,0:T(8,128)S(1)} %collective-permute-done.1, f32[2,640,640]{1,2,0:T(8,128)S(1)} %fusion.2, f32[2,640,640]{2,1,0:T(8,128)S(1)} %fusion.3, f32[2,640,640]{1,2,0:T(8,128)S(1)} %fusion.5, f32[640,640]{0,1:T(8,128)S(1)} %copy-done.1, f32[2,640,640]{2,1,0:T(8,128)S(1)} %copy-done.2), kind=kOutput, calls=%fused_computation.2 | convolution fusion | flops 3149004800 | bytes 19660800 | tf_op jit(solution)/shard_map/ab,rbd->rad/dot_general | solution.py:37
  400.8 3.0 copy.11
  (1 shorter events, 0.0 us)
Async XLA Ops:
  6.5 167.2 %all-gather.5.cloned.1.call-start = ((), (), s32[]{:S(2)}) async-start(), calls=%async_computation.1 | async-start | bytes 3481600 | tf_op jit(solution)/shard_map/all_gather | solution.py:29
  8.2 256.1 %all-gather.3.cloned.1.call-start = ((), (), s32[]{:S(2)}) async-start(), calls=%async_computation | async-start | bytes 3481600 | tf_op jit(solution)/shard_map/all_gather | solution.py:28
  16.0 2.8 copy-start
  18.8 264.5 %collective-permute-start = (f32[2,640,640]{1,2,0:T(8,128)S(1)}, f32[2,640,640]{1,2,0:T(8,128)}, u32[]{:S(2)}, u32[]{:S(2)}) collective-permute-start(f32[2,640,640]{1,2,0:T(8,128)S(1)} %broadcast_multiply_fusion), channel_id=1, source_target_pairs={{1,16},{2,17},{3,18},{4,19},{5,20},{6,21},{7,22},{8,23},{9,24},{10... | collective-permute-start | bytes 9830408 | tf_op jit(solution)/shard_map/ppermute | solution.py:17
  264.3 9.7 %copy-start.3 = (f32[2,640,640]{2,1,0:T(8,128)S(1)}, f32[2,640,640]{2,1,0:T(8,128)}, u32[]{:S(2)}) copy-start(f32[2,640,640]{2,1,0:T(8,128)} %all-gather.5.cloned.1.call-done) | copy-start | bytes 9830404
  271.6 6.9 %copy-start.2 = (f32[2,640,640]{2,1,0:T(8,128)S(1)}, f32[2,640,640]{2,1,0:T(8,128)}, u32[]{:S(2)}) copy-start(f32[2,640,640]{2,1,0:T(8,128)} %all-gather.3.cloned.1.call-done) | copy-start | bytes 9830404
  271.6 124.0 %collective-permute-start.1 = (f32[2,640,640]{1,2,0:T(8,128)S(1)}, f32[2,640,640]{1,2,0:T(8,128)S(1)}, u32[]{:S(2)}, u32[]{:S(2)}) collective-permute-start(f32[2,640,640]{1,2,0:T(8,128)S(1)} %convolution_bitcast_fusion), channel_id=1, source_target_pairs={{16,1},{17,2},{18,3},{19,4},{20,5},{21,6},{22,7},{23,8},{24,9},{25... | collective-permute-start | bytes 9830408 | tf_op jit(solution)/shard_map/ppermute | solution.py:17
  283.3 112.3 %copy-start.1 = (f32[640,640]{0,1:T(8,128)S(1)}, f32[640,640]{0,1:T(8,128)}, u32[]{:S(2)}) copy-start(f32[640,640]{0,1:T(8,128)} %copy-done) | copy-start | bytes 4915204
Sparse Core Ops, SparseCore 0:
  9.1 164.5 all-gather.4
  176.4 87.7 all-gather.2
where the time goes:
time: 411 us
  waiting for transfers between devices  339 us (82%)
  matrix products  35.9 us (9%)
  between operations  14.8 us (4%)
  local copies, waits for them, and re-layouts  7.54 us (2%)
  starting transfers between devices  7.2 us (2%)
  other arithmetic  6.25 us (2%)
    all_gather x1, waiting for transfers between devices, on_device(): lax.all_gather(jnp.concatenate([right_env, right_op]), 'lsec', axis=1, ti...  150 us
    ppermute x2, waiting for transfers between devices, shifted(): return lax.ppermute(value, ('lsec', 'rsec'), pairs)  106 us
    all_gather x1, waiting for transfers between devices, on_device(): lax.all_gather(jnp.concatenate([left_env, left_op]), 'rsec', axis=1, tile...  83.2 us
  transfers between devices with their start and end apart: 4, of which 3 were waited for; matrix products, arithmetic and copies ran while one was open for 10% of the time, Pallas kernels for 0%

commit v1 on v0

--- a/solution.py
+++ b/solution.py
@@ -26,7 +26,15 @@
     masked = states * mask[None]
     moved = shifted(masked, 1)
     left = lax.all_gather(jnp.concatenate([left_env, left_op]), "rsec", axis=1, tiled=True)
-    right = lax.all_gather(jnp.concatenate([right_env, right_op]), "lsec", axis=1, tiled=True)
+    right = jnp.concatenate(
+        lax.all_to_all(
+            jnp.stack([jnp.concatenate([right_env, right_op])] * lax.axis_size("lsec")),
+            "lsec",
+            0,
+            0,
+        ),
+        axis=1,
+    )
     env_l, oper_l, env_r, oper_r = (left[0], left[1], right[0], right[1])
     right_part = jnp.einsum("rbc,cd->rbd", masked, oper_r, precision=HI)
     source = jnp.einsum("ba,rbd->rad", oper_l, right_part, precision=HI)

time: 411 us -> 324 us (0.79)
  the two profiles are of different devices: /device:TPU:198 before, /device:TPU:251 now
where the time goes in v1:
time: 324 us; the launch traced here: 323 us
  waiting for transfers between devices  242 us (75%)
  matrix products  34.6 us (11%)
  between operations  14.9 us (5%)
  starting transfers between devices  14.7 us (5%)
  local copies, waits for them, and re-layouts  12.4 us (4%)
  other arithmetic  4.63 us (1%)
    ppermute x2, waiting for transfers between devices, shifted(): return lax.ppermute(value, ('lsec', 'rsec'), pairs)  125 us
    all_to_all x1, waiting for transfers between devices, on_device(): lax.all_to_all(jnp.stack([jnp.concatenate([right_env, right_op])] * lax.a...  62.5 us
    all_gather x1, waiting for transfers between devices, on_device(): lax.all_gather(jnp.concatenate([left_env, left_op]), 'rsec', axis=1, tile...  54.7 us
    ppermute x2, starting transfers between devices, shifted(): return lax.ppermute(value, ('lsec', 'rsec'), pairs)  7.46 us
    dot_general x1, matrix products, on_device(): source = jnp.einsum('ba,rbd->rad', oper_l, right_part, precision=HI)  7.27 us
    all_to_all x1, starting transfers between devices, on_device(): lax.all_to_all(jnp.stack([jnp.concatenate([right_env, right_op])] * lax.a...  7.25 us
    dot_general x1, matrix products, on_device(): inner = jnp.einsum('rbc,dc->rbd', moved, oper_r, precision=HI)  6.77 us
  transfers between devices with their start and end apart: 4, of which 3 were waited for; matrix products, arithmetic and copies ran while one was open for 12% of the time, Pallas kernels for 0%

profile of v1, /device:TPU:251, one launch (start us, length us, event | category | flops | bytes accessed | tf_op | source)
XLA Modules:
  0.0 323.3 jit_solution(251479620871344336)
XLA Ops:
  6.5 1.0 pad_maximum_fusion.1
  7.5 1.9 stack.2
  9.4 7.2 %all-to-all-start = ((f32[16,2,40,640]{3,2,1,0:T(8,128)}), f32[16,2,40,640]{3,2,1,0:T(8,128)}, u32[]{:S(2)}, u32[]{:S(2)}) async-start(f32[16,2,40,640]{3,2,1,0:T(8,128)} %stack.2), calls=%async_computation | async-start | bytes 6553600 | tf_op jit(solution)/shard_map/all_to_all | solution.py:30
  16.7 0.0 all-gather.2.cloned.1.call-start
  16.7 0.0 copy-done.7
  16.8 0.0 copy-done.8
  16.8 0.7 pad_maximum_fusion
  17.5 0.0 all-gather.2.cloned.1.call-update
  18.8 0.0 copy-done.6
  18.8 3.0 copy.12
  21.8 0.2 broadcast_multiply_fusion.1
  21.9 0.0 copy-start
  21.9 2.8 broadcast_multiply_fusion
  24.7 0.0 copy-done
  24.8 6.0 %collective-permute-start = (f32[2,640,640]{1,2,0:T(8,128)S(1)}, f32[2,640,640]{1,2,0:T(8,128)}, u32[]{:S(2)}, u32[]{:S(2)}) collective-permute-start(f32[2,640,640]{1,2,0:T(8,128)S(1)} %broadcast_multiply_fusion), channel_id=1, source_target_pairs={{1,16},{2,17},{3,18},{4,19},{5,20},{6,21},{7,22},{8,23},{9,24},{10... | collective-permute-start | bytes 9830408 | tf_op jit(solution)/shard_map/ppermute | solution.py:17
  30.7 62.5 %all-to-all-done = f32[16,2,40,640]{3,2,1,0:T(8,128)} async-done(((f32[16,2,40,640]{3,2,1,0:T(8,128)}), f32[16,2,40,640]{3,2,1,0:T(8,128)}, u32[]{:S(2)}, u32[]{:S(2)}) %all-to-all-start) | async-done | bytes 3276832 | tf_op jit(solution)/shard_map/all_to_all | solution.py:30
  93.2 3.3 %fusion.5 = (f32[1,16,40,640]{3,2,0,1:T(8,128)}, f32[1,16,40,640]{3,2,0,1:T(8,128)S(1)}) fusion(f32[2,16,40,640]{3,2,0,1:T(8,128)} %bitcast.5), kind=kLoop, calls=%fused_computation.16 | loop fusion | bytes 6553600 | tf_op jit(solution)/shard_map/slice | solution.py:38
  96.6 1.2 copy-done.2
  97.8 6.0 %fusion.8 = f32[2,640,640]{1,2,0:T(8,128)} fusion(f32[2,640,640]{1,2,0:T(8,128)S(1)} %broadcast_multiply_fusion, f32[640,640,1]{1,0,2:T(8,128)S(1)} %bitcast.41), kind=kOutput, calls=%fused_computation.19 | convolution fusion | flops 3145728000 | bytes 8192000 | tf_op jit(solution)/shard_map/rbc,cd->rbd/dot_general | solution.py:39
  103.8 54.7 %all-gather.2.cloned.1.call-done = f32[2,640,640]{2,1,0:T(8,128)} async-done(((f32[2,40,640]{2,1,0:T(8,128)}), f32[2,640,640]{2,1,0:T(8,128)}) %all-gather.2.cloned.1.call-update) | async-done | bytes 3276816 | tf_op jit(solution)/shard_map/all_gather | solution.py:28
  158.5 7.3 %convolution_bitcast_fusion = f32[2,640,640]{1,2,0:T(8,128)S(1)} fusion(f32[2,640,640]{1,2,0:T(8,128)} %fusion.8, f32[2,640,640]{2,1,0:T(8,128)} %all-gather.2.cloned.1.call-done), kind=kOutput, calls=%fused_computation.4 | convolution fusion | flops 3145728000 | bytes 8192000 | tf_op jit(solution)/shard_map/ba,rbd->rad/dot_general | solution.py:40
  165.8 1.5 collective-permute-start.1
  167.3 0.0 copy-done.5
  167.3 0.0 copy-start.4
  167.3 4.5 %fusion.6 = f32[2,640,640]{1,2,0:T(8,128)S(1)} fusion(f32[2,640,640]{1,2,0:T(8,128)S(1)} %broadcast_multiply_fusion, f32[640,640,1]{1,0,2:T(8,128)S(1)} %bitcast.43), kind=kOutput, calls=%fused_computation.17 | convolution fusion | flops 3145728000 | bytes 8192000 | tf_op jit(solution)/shard_map/rbc,dc->rbd/dot_general | solution.py:43
  171.8 0.0 copy-done.4
  171.8 4.8 %fusion.2 = f32[2,640,640]{2,1,0:T(8,128)S(1)} fusion(f32[2,640,640]{1,2,0:T(8,128)S(1)} %broadcast_multiply_fusion, f32[2,640,640]{2,1,0:T(8,128)S(1)} %copy-done.4), kind=kOutput, calls=%fused_computation.7 | convolution fusion | flops 3145728000 | bytes 8192000 | tf_op jit(solution)/shard_map/ab,rbc->rac/dot_general | solution.py:42
  176.6 0.0 collective-permute-done
  176.7 6.8 %fusion.7 = f32[2,640,640]{1,2,0:T(8,128)S(1)} fusion(f32[2,640,640]{1,2,0:T(8,128)} %collective-permute-done, f32[640,640,1]{1,0,2:T(8,128)S(1)} %bitcast.42), kind=kOutput, calls=%fused_computation.18 | convolution fusion | flops 3145728000 | bytes 8192000 | tf_op jit(solution)/shard_map/rbc,dc->rbd/dot_general | solution.py:44
  183.4 124.8 %collective-permute-done.1 = f32[2,640,640]{1,2,0:T(8,128)S(1)} collective-permute-done((f32[2,640,640]{1,2,0:T(8,128)S(1)}, f32[2,640,640]{1,2,0:T(8,128)S(1)}, u32[]{:S(2)}, u32[]{:S(2)}) %collective-permute-start.1) | collective-permute-done | bytes 3276832 | tf_op jit(solution)/shard_map/ppermute | solution.py:17
  308.3 5.2 %fusion.1 = f32[2,640,640]{1,2,0:T(8,128)S(1)} fusion(f32[2,640,640]{1,2,0:T(8,128)S(1)} %collective-permute-done.1, f32[2,640,640]{1,2,0:T(8,128)S(1)} %fusion.6, f32[2,640,640]{2,1,0:T(8,128)S(1)} %fusion.2, f32[2,640,640]{1,2,0:T(8,128)S(1)} %fusion.7, f32[640,640]{0,1:T(8,128)S(1)} %copy-done.1, f32[2,640,640]{2,1,0:T(8,128)S(1)} %copy-done.4), kind=kOutput, calls=%fused_computation.2 | convolution fusion | flops 3149004800 | bytes 19660800 | tf_op jit(solution)/shard_map/ab,rbd->rad/dot_general | solution.py:45
  313.5 3.0 copy.15
  (10 shorter events, 0.0 us)
Async XLA Ops:
  9.4 7.3 %copy-start.7 = (f32[1,40,640]{2,1,0:T(8,128)S(1)}, f32[1,40,640]{2,1,0:T(8,128)}, u32[]{:S(2)}) copy-start(f32[1,40,640]{2,1,0:T(8,128)} %param.10) | copy-start | bytes 307204
  9.4 7.3 %copy-start.8 = (f32[1,40,640]{2,1,0:T(8,128)S(1)}, f32[1,40,640]{2,1,0:T(8,128)}, u32[]{:S(2)}) copy-start(f32[1,40,640]{2,1,0:T(8,128)} %param.8) | copy-start | bytes 307204
  9.4 9.3 %copy-start.6 = (f32[2,640,640]{2,1,0:T(8,128)S(1)}, f32[2,640,640]{2,1,0:T(8,128)}, u32[]{:S(2)}) copy-start(f32[2,640,640]{2,1,0:T(8,128)} %param.7) | copy-start | bytes 9830404
  9.4 83.8 %all-to-all-start = ((f32[16,2,40,640]{3,2,1,0:T(8,128)}), f32[16,2,40,640]{3,2,1,0:T(8,128)}, u32[]{:S(2)}, u32[]{:S(2)}) async-start(f32[16,2,40,640]{3,2,1,0:T(8,128)} %stack.2), calls=%async_computation | async-start | bytes 6553600 | tf_op jit(solution)/shard_map/all_to_all | solution.py:30
  16.7 141.8 %all-gather.2.cloned.1.call-start = ((), (), s32[]{:S(2)}) async-start(), calls=%async_computation.1 | async-start | bytes 3481600 | tf_op jit(solution)/shard_map/all_gather | solution.py:28
  21.9 2.8 copy-start
  24.8 151.9 %collective-permute-start = (f32[2,640,640]{1,2,0:T(8,128)S(1)}, f32[2,640,640]{1,2,0:T(8,128)}, u32[]{:S(2)}, u32[]{:S(2)}) collective-permute-start(f32[2,640,640]{1,2,0:T(8,128)S(1)} %broadcast_multiply_fusion), channel_id=1, source_target_pairs={{1,16},{2,17},{3,18},{4,19},{5,20},{6,21},{7,22},{8,23},{9,24},{10... | collective-permute-start | bytes 9830408 | tf_op jit(solution)/shard_map/ppermute | solution.py:17
  96.6 1.2 copy-start.2
  158.5 8.8 %copy-start.5 = (f32[1,16,40,640]{3,2,0,1:T(8,128)S(1)}, f32[1,16,40,640]{3,2,0,1:T(8,128)}, u32[]{:S(2)}) copy-start(f32[1,16,40,640]{3,2,0,1:T(8,128)} %get-tuple-element.5) | copy-start | bytes 4915204
  165.8 142.5 %collective-permute-start.1 = (f32[2,640,640]{1,2,0:T(8,128)S(1)}, f32[2,640,640]{1,2,0:T(8,128)S(1)}, u32[]{:S(2)}, u32[]{:S(2)}) collective-permute-start(f32[2,640,640]{1,2,0:T(8,128)S(1)} %convolution_bitcast_fusion), channel_id=1, source_target_pairs={{16,1},{17,2},{18,3},{19,4},{20,5},{21,6},{22,7},{23,8},{24,9},{25... | collective-permute-start | bytes 9830408 | tf_op jit(solution)/shard_map/ppermute | solution.py:17
  167.3 4.5 %copy-start.4 = (f32[2,640,640]{2,1,0:T(8,128)S(1)}, f32[2,640,640]{2,1,0:T(8,128)}, u32[]{:S(2)}) copy-start(f32[2,640,640]{2,1,0:T(8,128)} %all-gather.2.cloned.1.call-done) | copy-start | bytes 9830404
  171.8 4.9 %copy-start.3 = (f32[1,16,40,640]{3,2,0,1:T(8,128)S(1)}, f32[1,16,40,640]{3,2,0,1:T(8,128)}, u32[]{:S(2)}) copy-start(f32[1,16,40,640]{3,2,0,1:T(8,128)} %copy-done.2) | copy-start | bytes 4915204
  176.6 131.6 %copy-start.1 = (f32[640,640]{0,1:T(8,128)S(1)}, f32[640,640]{0,1:T(8,128)}, u32[]{:S(2)}) copy-start(f32[640,640]{0,1:T(8,128)} %copy-done) | copy-start | bytes 4915204
Sparse Core Ops, SparseCore 0:
  20.3 138.1 all-gather.1
